TPU v7x, 32 devices: a whole 2x2x4 slice. The times are simulated.
32 devices in a mesh: dev: 32 (over z, y, x, core).
Axes of the slice: x: 2, y: 2, z: 4, core: 2. Of those that a mesh axis runs over, the one named last changes fastest.
Arguments:
- peripheral: bfloat16 [131072, 256], P('dev'), may hold values from -6 to 6
- hubs: bfloat16 [2048, 256], P('dev'), may hold values from -6 to 6
- tiles: bfloat16 [4608, 128, 128], P('dev'), may hold values from -0.5 to 0.5
- tile_rows: int32 [4608], P('dev'), may hold values from 0 to 1039, as said below
- local_cols: int32 [3584], P('dev'), may hold values from 0 to 1039, as said below
- tile_count: int32 [32], P('dev'), may hold values from 32 to 144, as said below
- send_list: int32 [32, 32], P('dev'), may hold values from 0 to 31
- hub_place: int32 [2048], replicated, may hold values from 0 to 2047, each once
- w_in: bfloat16 [2, 256, 2048], replicated, may hold values from -0.375 to 0.375
- w_out: bfloat16 [2, 2048, 256], replicated, may hold values from -0.125 to 0.125
Outputs:
- peripheral_out: bfloat16 [131072, 256], P('dev')
- hubs_out: bfloat16 [2048, 256], P('dev')
Inputs may be any that keep to these rules, and one draw needn't show every extreme that they name: `tile_rows`: row blocks of device d's slots are hub blocks (below 16) or d's own blocks 16 + d * 32 to 16 + d * 32 + 31; slots below 32 always name an own block. `local_cols`: column blocks of device d's slots from 32 on are hub blocks or d's own blocks. `tile_count`: every device holds at least 32 live slots; some device is full in every draw.
All inputs are finite; a program needn't handle non-finite values.
Results may differ from a plain program's by a relative error of at most 0.005.
Values may be sent and summed in bfloat16 or wider, within the bound.
No kernel may reach another device: no remote copies, remote signals or barrier semaphores. Data moves between devices by JAX's collectives and lax.ppermute only.
A program may use at most 128 MiB of HBM per device.

v0:
```python
import jax
import jax.numpy as jnp
from jax import lax
from jax.sharding import PartitionSpec as P

epsilon = 1e-06


def feed_forward(rows_in, summed, first, second):
    united = rows_in.astype(jnp.float32) + summed
    normed = (
        united * lax.rsqrt(jnp.mean(united * united, axis=-1, keepdims=True) + epsilon)
    ).astype(jnp.bfloat16)
    hidden = jnp.maximum(jnp.dot(normed, first, preferred_element_type=jnp.float32), 0.0).astype(
        jnp.bfloat16
    )
    return (united + jnp.dot(hidden, second, preferred_element_type=jnp.float32)).astype(
        jnp.bfloat16
    )


def body(
    peripheral, hubs, tiles, tile_rows, local_cols, tile_count, send_list, hub_place, w_in, w_out
):
    devices = lax.axis_size("dev")
    position = lax.axis_index("dev")
    capacity = tiles.shape[0]
    block_size = tiles.shape[1]
    width = peripheral.shape[1]
    own_count = peripheral.shape[0] // block_size
    hub_count = hub_place.shape[0] // block_size
    hub_local = hubs.shape[0]
    peri_local = peripheral.shape[0]
    targets = hub_count + own_count
    slot_index = jnp.arange(capacity, dtype=jnp.int32)
    live_slot = (slot_index < tile_count[0]).astype(jnp.float32)
    row_local = jnp.where(tile_rows < hub_count, tile_rows, tile_rows - position * own_count)
    cols_own = jnp.where(local_cols < hub_count, local_cols, local_cols - position * own_count)
    inverse = jnp.argsort(hub_place)
    peri_rows = peripheral
    hub_own = hubs
    hub_full = lax.all_gather(hubs, "dev", axis=0, tiled=True)
    layers = w_in.shape[0]
    for layer_index in range(layers):
        hub_global = hub_full[hub_place].reshape(hub_count, block_size, width)
        own_blocks = peri_rows.reshape(own_count, block_size, width)
        outgoing = own_blocks[send_list[0]]
        empty = jnp.zeros((targets, block_size, width), jnp.float32)
        incoming = lax.all_to_all(outgoing, "dev", split_axis=0, concat_axis=0, tiled=True)
        column_table = jnp.concatenate([hub_global, own_blocks, incoming], axis=0)
        col_index = jnp.concatenate(
            [hub_count + own_count + jnp.arange(devices, dtype=jnp.int32), cols_own]
        )

        def group_step(group, carry):
            start = 0 + group * 16
            tile_group = lax.dynamic_slice_in_dim(tiles, start, 16, 0)
            col_group = lax.dynamic_slice_in_dim(col_index, start, 16, 0)
            row_group = lax.dynamic_slice_in_dim(row_local, start, 16, 0)
            live_group = lax.dynamic_slice_in_dim(live_slot, start, 16, 0)
            products = jnp.einsum(
                "tij,tjf->tif",
                tile_group,
                column_table[col_group],
                preferred_element_type=jnp.float32,
            )
            return carry.at[row_group].add(products * live_group[:, None, None])

        summed = lax.fori_loop(0, capacity // 16, group_step, empty)
        hub_part = summed[:hub_count].reshape(hub_count * block_size, width)[inverse]
        peri_sum = summed[hub_count:].reshape(peri_local, width)
        first, second = (w_in[layer_index], w_out[layer_index])
        hub_sum = lax.psum(hub_part, "dev")
        if layer_index + 1 < layers:
            updated = feed_forward(
                jnp.concatenate([peri_rows, hub_full], axis=0),
                jnp.concatenate([peri_sum, hub_sum], axis=0),
                first,
                second,
            )
            peri_rows = updated[:peri_local]
            hub_full = updated[peri_local:]
        else:
            mine = lax.dynamic_slice_in_dim(hub_full, position * hub_local, hub_local, 0)
            mine_sum = lax.dynamic_slice_in_dim(hub_sum, position * hub_local, hub_local, 0)
            updated = feed_forward(
                jnp.concatenate([peri_rows, mine], axis=0),
                jnp.concatenate([peri_sum, mine_sum], axis=0),
                first,
                second,
            )
            peri_rows = updated[:peri_local]
            hub_own = updated[peri_local:]
    return (peri_rows, hub_own)


def solution(mesh):
    in_specs = (
        P("dev", None),
        P("dev", None),
        P("dev", None, None),
        P("dev"),
        P("dev"),
        P("dev"),
        P("dev", None),
        P(),
        P(),
        P(),
    )
    out_specs = (P("dev", None), P("dev", None))
    return jax.shard_map(body, mesh=mesh, in_specs=in_specs, out_specs=out_specs, check_vma=False)
```

profile of v0, /device:TPU:0, one launch (start us, length us, event | category | flops | bytes accessed | tf_op | source)
XLA Modules:
  0.0 677.5 jit_solution(4452366558562363239)
XLA Ops:
  11.5 7.4 %all-to-all-start = ((bf16[32,128,256]{2,1,0:T(8,128)(2,1)}), bf16[32,128,256]{2,1,0:T(8,128)(2,1)}, u32[]{:S(2)}, u32[]{:S(2)}) async-start(bf16[32,128,256]{2,1,0:T(8,128)(2,1)} %gather_fusion.3), calls=%async_computation | async-start | bytes 4194304 | tf_op jit(solution)/shard_map/all_to_all | solution.py:49
  20.4 5.0 sort.17
  25.5 58.5 %all-gather.2.cloned.1.call-done = bf16[2048,256]{1,0:T(8,128)(2,1)} async-done(((bf16[64,256]{1,0:T(8,128)(2,1)}), bf16[2048,256]{1,0:T(8,128)(2,1)}) %all-gather.2.cloned.1.call-update) | async-done | bytes 1048592 | tf_op jit(solution)/shard_map/all_gather | solution.py:42
  84.0 8.0 %gather_fusion.2 = bf16[2048,256]{1,0:T(8,128)(2,1)S(1)} fusion(bf16[2048,256]{1,0:T(8,128)(2,1)} %all-gather.2.cloned.1.call-done, s32[2048]{0:T(1024)S(1)} %fusion.27), kind=kCustom, calls=%fused_computation.2 | custom fusion | bytes 2105344 | tf_op jit(solution)/shard_map/gather | solution.py:45
  99.9 83.3 %while.26 = (s32[]{:T(128)}, f32[48,128,256]{2,1,0:T(8,128)}, s32[144]{0:T(256)S(1)}, bf16[144,128,128]{2,1,0:T(8,128)(2,1)}, s32[144]{0:T(256)S(1)}, /*index=5*...) while((s32[]{:T(128)}, f32[48,128,256]{2,1,0:T(8,128)}, ...), condition=%wide.region_2.3_spmd, body=%wide.region_0.2_spmd.sunk | while | flops 135267424 | bytes 12063527 | solution.py:69
  104.6 4.5 scatter_fusion
  141.6 4.6 scatter_fusion
  150.9 4.6 scatter_fusion
  185.0 8.6 %gather_fusion.4 = f32[2048,256]{1,0:T(8,128)} fusion(f32[2048,256]{1,0:T(8,128)S(1)} %bitcast.35, s32[2048]{0:T(1024)S(1)} %fusion.28), kind=kCustom, calls=%fused_computation.4 | custom fusion | bytes 4202496 | tf_op jit(solution)/shard_map/gather | solution.py:70
  193.6 4.9 slice.36
  198.5 128.2 %all-reduce.3.cloned.1.call-done = f32[2048,256]{1,0:T(8,128)} async-done(((f32[2048,256]{1,0:T(8,128)}), f32[2048,256]{1,0:T(8,128)}) %all-reduce.3.cloned.1.call-update) | async-done | bytes 2097168 | tf_op jit(solution)/shard_map/psum | solution.py:73
  330.5 23.7 %fusion.9 = bf16[6144,256]{1,0:T(8,128)(2,1)} fusion(f32[2048,256]{1,0:T(8,128)} %all-reduce.3.cloned.1.call-done, f32[4096,256]{1,0:T(8,128)} %bitcast.43, f32[6144]{0:T(1024)S(1)} %add_rsqrt_fusion, bf16[2048,256]{1,0:T(8,128)(2,1)S(1)} %copy-done.1, bf16[4096,256]{1,0:T(8,128)(2,1)S(1)} %copy-done.5, bf16[2,2048,256]{2,1,0:T(8,128)(2,1)} %param.23, ...), kind=kOutput, calls=%fused_computation.28 | convolution fusion | flops 12935233536 | bytes 24141824 | tf_op jit(solution)/shard_map/dot_general | solution.py:17
  362.9 9.2 %gather_fusion.5 = bf16[2048,256]{1,0:T(8,128)(2,1)} fusion(bf16[2048,256]{1,0:T(8,128)(2,1)S(1)} %slice.65, s32[2048]{0:T(1024)S(1)} %fusion.27), kind=kCustom, calls=%fused_computation.5 | custom fusion | bytes 2105344 | tf_op jit(solution)/shard_map/gather | solution.py:45
  372.1 38.3 %all-to-all-done.1 = bf16[32,128,256]{2,1,0:T(8,128)(2,1)} async-done(((bf16[32,128,256]{2,1,0:T(8,128)(2,1)}), bf16[32,128,256]{2,1,0:T(8,128)(2,1)}, u32[]{:S(2)}, u32[]{:S(2)}) %all-to-all-start.1) | async-done | bytes 2097184 | tf_op jit(solution)/shard_map/all_to_all | solution.py:49
  410.5 4.8 pad_maximum_fusion.1
  418.7 83.4 %while.27 = (s32[]{:T(128)}, f32[48,128,256]{2,1,0:T(8,128)}, s32[144]{0:T(256)S(1)}, bf16[144,128,128]{2,1,0:T(8,128)(2,1)}, s32[144]{0:T(256)S(1)}, /*index=5*...) while((s32[]{:T(128)}, f32[48,128,256]{2,1,0:T(8,128)}, ...), condition=%wide.region_8.9_spmd, body=%wide.region_6.8_spmd.sunk | while | flops 135267424 | bytes 12063527 | solution.py:69
  432.7 4.5 scatter_fusion.1
  451.1 4.6 scatter_fusion.1
  460.4 4.6 scatter_fusion.1
  469.7 4.6 scatter_fusion.1
  503.9 8.6 %gather_fusion.7 = f32[2048,256]{1,0:T(8,128)} fusion(f32[2048,256]{1,0:T(8,128)S(1)} %bitcast.34, s32[2048]{0:T(1024)S(1)} %fusion.28), kind=kCustom, calls=%fused_computation.7 | custom fusion | bytes 4202496 | tf_op jit(solution)/shard_map/gather | solution.py:70
  513.3 4.9 slice.42
  518.1 127.7 %all-reduce.5.cloned.1.call-done = f32[2048,256]{1,0:T(8,128)} async-done(((f32[2048,256]{1,0:T(8,128)}), f32[2048,256]{1,0:T(8,128)}) %all-reduce.5.cloned.1.call-update) | async-done | bytes 2097168 | tf_op jit(solution)/shard_map/psum | solution.py:73
  649.6 16.9 %fusion.10 = bf16[4160,256]{1,0:T(8,128)(2,1)} fusion(f32[64,256]{1,0:T(8,128)S(1)} %constant_dynamic-slice_fusion, f32[4096,256]{1,0:T(8,128)} %bitcast.41, f32[4160]{0:T(1024)S(1)} %add_rsqrt_fusion.1, bf16[64,256]{1,0:T(8,128)(2,1)S(1)} %constant_dynamic-slice_fusion.1, bf16[4096,256]{1,0:T(8,128)(2,1)S(1)} %copy-done.3, ...), kind=kOutput, calls=%fused_computation.30 | convolution fusion | flops 8758231040 | bytes 17027072 | tf_op jit(solution)/shard_map/dot_general | solution.py:17
  (153 shorter events, 175.9 us)
Async XLA Ops:
  7.8 12.5 %copy-start.6 = (s32[2048]{0:T(1024)S(1)}, s32[2048]{0:T(1024)}, u32[]{:S(2)}) copy-start(s32[2048]{0:T(1024)} %param.21) | copy-start | bytes 24580
  7.8 17.6 %copy-start.8 = (s32[112]{0:T(128)S(1)}, s32[112]{0:T(128)}, u32[]{:S(2)}) copy-start(s32[112]{0:T(128)} %param.18) | copy-start | bytes 1348
  7.8 17.6 %copy-start.7 = (s32[144]{0:T(256)S(1)}, s32[144]{0:T(256)}, u32[]{:S(2)}) copy-start(s32[144]{0:T(256)} %param.17) | copy-start | bytes 1732
  11.5 80.6 %all-to-all-start = ((bf16[32,128,256]{2,1,0:T(8,128)(2,1)}), bf16[32,128,256]{2,1,0:T(8,128)(2,1)}, u32[]{:S(2)}, u32[]{:S(2)}) async-start(bf16[32,128,256]{2,1,0:T(8,128)(2,1)} %gather_fusion.3), calls=%async_computation | async-start | bytes 4194304 | tf_op jit(solution)/shard_map/all_to_all | solution.py:49
  18.9 65.1 %all-gather.2.cloned.1.call-start = ((), (), s32[]{:S(2)}) async-start(), calls=%async_computation.2 | async-start | bytes 1081344 | tf_op jit(solution)/shard_map/all_gather | solution.py:42
  19.6 307.1 %all-reduce.3.cloned.1.call-start = ((), (), s32[]{:S(2)}) async-start(), calls=%async_computation.3 | async-start | bytes 4194304 | tf_op jit(solution)/shard_map/psum | solution.py:73
  25.5 66.5 %copy-start.4 = (bf16[4096,256]{1,0:T(8,128)(2,1)S(1)}, bf16[4096,256]{1,0:T(8,128)(2,1)}, u32[]{:S(2)}) copy-start(bf16[4096,256]{1,0:T(8,128)(2,1)} %param.14) | copy-start | bytes 6291460
  193.6 133.1 %copy-start.1 = (bf16[2048,256]{1,0:T(8,128)(2,1)S(1)}, bf16[2048,256]{1,0:T(8,128)(2,1)}, u32[]{:S(2)}) copy-start(bf16[2048,256]{1,0:T(8,128)(2,1)} %all-gather.2.cloned.1.call-done) | copy-start | bytes 3145732
  193.6 133.1 %copy-start.5 = (bf16[4096,256]{1,0:T(8,128)(2,1)S(1)}, bf16[4096,256]{1,0:T(8,128)(2,1)}, u32[]{:S(2)}) copy-start(bf16[4096,256]{1,0:T(8,128)(2,1)} %param.14) | copy-start | bytes 6291460
  355.9 54.5 %copy-start.2 = (bf16[4096,256]{1,0:T(8,128)(2,1)}, bf16[4096,256]{1,0:T(8,128)(2,1)S(1)}, u32[]{:S(2)}) copy-start(bf16[4096,256]{1,0:T(8,128)(2,1)S(1)} %slice.64) | copy-start | bytes 6291460
  358.0 52.5 %all-to-all-start.1 = ((bf16[32,128,256]{2,1,0:T(8,128)(2,1)}), bf16[32,128,256]{2,1,0:T(8,128)(2,1)}, u32[]{:S(2)}, u32[]{:S(2)}) async-start(bf16[32,128,256]{2,1,0:T(8,128)(2,1)} %gather_fusion.6), calls=%async_computation.1 | async-start | bytes 4194304 | tf_op jit(solution)/shard_map/all_to_all | solution.py:49
  361.6 284.3 %all-reduce.5.cloned.1.call-start = ((), (), s32[]{:S(2)}) async-start(), calls=%async_computation.4 | async-start | bytes 4194304 | tf_op jit(solution)/shard_map/psum | solution.py:73
  362.9 9.2 %copy-start = (bf16[2048,256]{1,0:T(8,128)(2,1)}, bf16[2048,256]{1,0:T(8,128)(2,1)S(1)}, u32[]{:S(2)}) copy-start(bf16[2048,256]{1,0:T(8,128)(2,1)S(1)} %slice.65) | copy-start | bytes 3145732
  513.3 133.4 %copy-start.3 = (bf16[4096,256]{1,0:T(8,128)(2,1)S(1)}, bf16[4096,256]{1,0:T(8,128)(2,1)}, u32[]{:S(2)}) copy-start(bf16[4096,256]{1,0:T(8,128)(2,1)} %copy-done.2) | copy-start | bytes 6291460
Sparse Core Ops, SparseCore 0:
  22.6 61.3 all-gather.1
  193.7 132.9 all-reduce.2
  512.6 133.2 all-reduce.4
where the time goes:
time: 680 us; the launch traced here: 678 us
  waiting for transfers between devices  353 us (52%)
  local copies, waits for them, and re-layouts  126 us (19%)
  other arithmetic  105 us (15%)
  matrix products  67 us (10%)
  between operations  14.6 us (2%)
  starting transfers between devices  11.2 us (2%)
    psum x2, waiting for transfers between devices, body(): hub_sum = lax.psum(hub_part, 'dev')  256 us
    scatter-add x18, other arithmetic, group_step(): return carry.at[row_group].add(products * live_group[:, None, None])  81.4 us
    all_gather x1, waiting for transfers between devices, body(): hub_full = lax.all_gather(hubs, 'dev', axis=0, tiled=True)  58.5 us
    gather x18, local copies, waits for them, and re-layouts, group_step(): column_table[col_group]  55.8 us
    dot_general x2, matrix products, feed_forward(): jnp.dot(hidden, second, preferred_element_type=jnp.float32)  40.7 us
    all_to_all x2, waiting for transfers between devices, body(): lax.all_to_all(outgoing, 'dev', split_axis=0, concat_axis=0, tiled=True)  38.4 us
    dot_general x18, matrix products, group_step(): jnp.einsum('tij,tjf->tif', tile_group, column_table[col_group], preferred...  26.4 us
    gather x2, local copies, waits for them, and re-layouts, body(): summed[:hub_count].reshape(hub_count * block_size, width)[inverse]  17.2 us
  transfers between devices with their start and end apart: 5, of which 4 were waited for; matrix products, arithmetic and copies ran while one was open for 5% of the time, Pallas kernels for 0%

commit v1 on v0

v1 whole, which is shorter than its diff:
```python
import functools

import jax
import jax.numpy as jnp
from jax import lax
from jax.experimental import pallas as pl
from jax.experimental.pallas import tpu as pltpu
from jax.sharding import PartitionSpec as P

epsilon = 1e-06
f32 = jnp.float32
bf16 = jnp.bfloat16
MIB = 1024 * 1024
VMEM = pl.BlockSpec(memory_space=pltpu.VMEM)
SMEM = pl.BlockSpec(memory_space=pltpu.SMEM)
ANY = pl.BlockSpec(memory_space=pl.ANY)


def dot(a, b):
    return jnp.dot(a, b, preferred_element_type=f32)


def params(mib):
    return pltpu.CompilerParams(vmem_limit_bytes=mib * MIB)


def normalise(u):
    return (u * lax.rsqrt(jnp.mean(u * u, axis=-1, keepdims=True) + epsilon)).astype(bf16)


def network(u, first, second, hidden_step):
    normed = normalise(u)
    total = u
    for start in range(0, first.shape[-1], hidden_step):
        cut = slice(start, start + hidden_step)
        hidden = jnp.maximum(dot(normed, first[:, cut]), 0.0).astype(bf16)
        total = total + dot(hidden, second[cut, :])
    return total.astype(bf16)


def listed_slots(rows, cols, count, picked, begin, hub_count, want_hub):
    def step(slot, found):
        picked[found] = slot
        is_hub = (rows[slot] < hub_count).astype(jnp.int32)
        return found + (is_hub if want_hub else 1 - is_hub)

    return lax.fori_loop(begin, count[0], step, jnp.int32(0))


def add_products(rows, cols, picked, found, begin, tiles, table, total, row_shift, spare, group):
    def step(number, unused):
        where, products = [], []
        for lane in range(group):
            place = number * group + lane
            live = place < found
            slot = picked[jnp.minimum(place, found - 1)]
            where.append(jnp.where(live, rows[slot] - row_shift, spare))
            products.append(dot(tiles[slot], table[cols[slot - begin]]))
        for row, product in zip(where, products):
            total[row] += product
        return unused

    lax.fori_loop(0, (found + group - 1) // group, step, 0)


def place_rows(place_col, source, out):
    count = source.shape[0]
    step = 256

    def rows_step(number, unused):
        cut = pl.ds(pl.multiple_of(number * step, step), step)
        lanes = lax.broadcasted_iota(jnp.int32, (step, count), 1)
        unit = jnp.where(place_col[cut, :] == lanes, 1.0, 0.0).astype(bf16)
        out[cut, :] = dot(unit, source[...]).astype(bf16)
        return unused

    lax.fori_loop(0, count // step, rows_step, 0)


def pack_kernel(chosen, blocks, outgoing, sems):
    copies = []
    for number in range(outgoing.shape[0]):
        copy = pltpu.make_async_copy(
            blocks.at[chosen[0, number]], outgoing.at[number], sems.at[number]
        )
        copy.start()
        copies.append(copy)
    for copy in copies:
        copy.wait()


def pack(chosen, blocks):
    devices = chosen.shape[1]
    return pl.pallas_call(
        pack_kernel,
        out_shape=jax.ShapeDtypeStruct((devices,) + blocks.shape[1:], bf16),
        in_specs=[SMEM, ANY],
        out_specs=ANY,
        scratch_shapes=[pltpu.SemaphoreType.DMA((devices,))],
        name="pack",
    )(chosen, blocks)


def hub_first_kernel(rows, cols, count, place_col, gathered, own, tiles, part, table, total, picked):
    hub_count, block_size, width = part.shape
    begin = tiles.shape[0] - cols.shape[0]
    flat = table.at[pl.ds(0, hub_count)].reshape(hub_count * block_size, width)
    place_rows(place_col, gathered, flat)
    table[hub_count:] = own[...]
    total[...] = jnp.zeros_like(total)
    found = listed_slots(rows, cols, count, picked, begin, hub_count, True)
    add_products(rows, cols, picked, found, begin, tiles, table, total, 0, hub_count, 4)
    part[...] = total[:hub_count].astype(bf16)


def hub_first(rows, cols, count, place_col, gathered, own, tiles):
    block_size, width = own.shape[1:]
    hub_count = gathered.shape[0] // block_size
    targets = hub_count + own.shape[0]
    return pl.pallas_call(
        hub_first_kernel,
        out_shape=(
            jax.ShapeDtypeStruct((hub_count, block_size, width), bf16),
            jax.ShapeDtypeStruct((targets, block_size, width), bf16),
        ),
        in_specs=[SMEM, SMEM, SMEM, VMEM, VMEM, VMEM, VMEM],
        out_specs=(VMEM, VMEM),
        scratch_shapes=[
            pltpu.VMEM((hub_count + 1, block_size, width), f32),
            pltpu.SMEM((rows.shape[0],), jnp.int32),
        ],
        compiler_params=params(50),
        name="hub_first",
    )(rows, cols, count, place_col, gathered, own, tiles)


def hub_second_kernel(rows, cols, count, mine_rows, place_row, hubs, own, tiles, part, mine, table, total, picked):
    hub_count, block_size, width = hubs.shape
    begin = tiles.shape[0] - cols.shape[0]
    hub_rows = hub_count * block_size
    table[:hub_count] = hubs[...]
    table[hub_count:] = own[...]
    total[...] = jnp.zeros_like(total)
    found = listed_slots(rows, cols, count, picked, begin, hub_count, True)
    add_products(rows, cols, picked, found, begin, tiles, table, total, 0, hub_count, 4)
    sums = total[:hub_count].astype(bf16).reshape(hub_rows, width)
    step = 256

    def rows_step(number, unused):
        cut = pl.ds(pl.multiple_of(number * step, step), step)
        down = lax.broadcasted_iota(jnp.int32, (step, hub_rows), 0) + number * step
        unit = jnp.where(place_row[...] == down, 1.0, 0.0).astype(bf16)
        part[cut, :] = dot(unit, sums).astype(bf16)
        return unused

    lax.fori_loop(0, hub_rows // step, rows_step, 0)
    own_rows = mine.shape[0]
    down = lax.broadcasted_iota(jnp.int32, (own_rows, hub_rows), 0) + mine_rows[0]
    unit = jnp.where(place_row[...] == down, 1.0, 0.0).astype(bf16)
    mine[...] = dot(unit, hubs[...].reshape(hub_rows, width)).astype(bf16)


def hub_second(rows, cols, count, mine_rows, place_row, hubs, own, tiles, hub_local):
    hub_count, block_size, width = hubs.shape
    targets = hub_count + own.shape[0]
    return pl.pallas_call(
        hub_second_kernel,
        out_shape=(
            jax.ShapeDtypeStruct((hub_count * block_size, width), bf16),
            jax.ShapeDtypeStruct((hub_local, width), bf16),
            jax.ShapeDtypeStruct((targets, block_size, width), bf16),
        ),
        in_specs=[SMEM, SMEM, SMEM, SMEM, VMEM, VMEM, VMEM, VMEM],
        out_specs=(VMEM, VMEM, VMEM),
        scratch_shapes=[
            pltpu.VMEM((hub_count + 1, block_size, width), f32),
            pltpu.SMEM((rows.shape[0],), jnp.int32),
        ],
        compiler_params=params(50),
        name="hub_second",
    )(rows, cols, count, mine_rows, place_row, hubs, own, tiles)


def own_kernel(rows, cols, count, table, tiles, total, scratch, picked):
    own_count = total.shape[0]
    hub_count = table.shape[0] - own_count
    begin = tiles.shape[0] - cols.shape[0]
    scratch[:own_count] = table[hub_count:].astype(f32)
    found = listed_slots(rows, cols, count, picked, begin, hub_count, False)
    add_products(
        rows, cols, picked, found, begin, tiles, table, scratch, hub_count, own_count, 4
    )
    total[...] = scratch[:own_count]


def own_sums(rows, cols, count, table, tiles, own_count):
    block_size, width = table.shape[1:]
    return pl.pallas_call(
        own_kernel,
        out_shape=jax.ShapeDtypeStruct((own_count, block_size, width), f32),
        in_specs=[SMEM, SMEM, SMEM, VMEM, VMEM],
        out_specs=VMEM,
        scratch_shapes=[
            pltpu.VMEM((own_count + 1, block_size, width), f32),
            pltpu.SMEM((rows.shape[0],), jnp.int32),
        ],
        compiler_params=params(50),
        name="own_sums",
    )(rows, cols, count, table, tiles)


def hub_network_kernel(rows_in, summed, first, second, out):
    u = rows_in[...].astype(f32) + summed[...]
    out[...] = network(u, first, second, first.shape[-1])


def hub_network(rows_in, summed, first, second):
    return pl.pallas_call(
        hub_network_kernel,
        out_shape=jax.ShapeDtypeStruct(rows_in.shape, bf16),
        in_specs=[VMEM] * 4,
        out_specs=VMEM,
        compiler_params=params(24),
        name="hub_network",
    )(rows_in, summed, first, second)


def network_kernel(row_step, with_send, rows, chosen, base, incoming, tiles, first, second, *refs):
    if with_send:
        out, outgoing, u, inc, adj, one, two, result, sems = refs
    else:
        out, u, inc, adj, one, two, result, sems = refs
        outgoing = None
    own_count, block_size, width = u.shape
    remote = incoming.shape[0]
    loads = [
        pltpu.make_async_copy(base, u, sems.at[0]),
        pltpu.make_async_copy(incoming, inc, sems.at[1]),
        pltpu.make_async_copy(tiles.at[pl.ds(0, remote)], adj, sems.at[2]),
        pltpu.make_async_copy(first, one, sems.at[3]),
        pltpu.make_async_copy(second, two, sems.at[4]),
    ]
    for load in loads:
        load.start()
    for load in loads[:3]:
        load.wait()
    group = 4

    def slots_step(number, unused):
        products = [
            dot(adj[number * group + lane], inc[number * group + lane]) for lane in range(group)
        ]
        for lane in range(group):
            u[rows[number * group + lane]] += products[lane]
        return unused

    lax.fori_loop(0, remote // group, slots_step, 0)
    for load in loads[3:]:
        load.wait()
    blocks = row_step // block_size
    steps = own_count // blocks

    def rows_step(number, unused):
        cut = pl.ds(number * blocks, blocks)
        values = u[cut].reshape(row_step, width)
        result[cut] = network(values, one, two, 512).reshape(blocks, block_size, width)
        return unused

    lax.fori_loop(0, steps, rows_step, 0)
    copies = [pltpu.make_async_copy(result, out, sems.at[0])]
    if with_send:
        for number in range(remote):
            copies.append(
                pltpu.make_async_copy(
                    result.at[chosen[0, number]], outgoing.at[number], sems.at[1 + number]
                )
            )
    for copy in copies:
        copy.start()
    for copy in copies:
        copy.wait()


def peripheral_network(rows, chosen, base, incoming, tiles, first, second, with_send):
    own_count, block_size, width = base.shape
    remote = incoming.shape[0]
    shapes = [jax.ShapeDtypeStruct(base.shape, bf16)]
    if with_send:
        shapes.append(jax.ShapeDtypeStruct(incoming.shape, bf16))
    return pl.pallas_call(
        functools.partial(network_kernel, 512, with_send),
        out_shape=tuple(shapes),
        in_specs=[SMEM, SMEM] + [ANY] * 5,
        out_specs=(ANY,) * len(shapes),
        scratch_shapes=[
            pltpu.VMEM(base.shape, f32),
            pltpu.VMEM(incoming.shape, bf16),
            pltpu.VMEM((remote,) + tiles.shape[1:], bf16),
            pltpu.VMEM(first.shape, bf16),
            pltpu.VMEM(second.shape, bf16),
            pltpu.VMEM(base.shape, bf16),
            pltpu.SemaphoreType.DMA((5 + remote,)),
        ],
        compiler_params=params(50),
        name="peripheral_network",
    )(rows, chosen, base, incoming, tiles, first, second)


def exchange(x, bit):
    devices = lax.axis_size("dev")
    return lax.ppermute(x, "dev", [(i, i ^ bit) for i in range(devices)])


def gather_step(x, bit):
    position = lax.axis_index("dev")
    other = exchange(x, bit)
    mine_first = jnp.stack([x, other], axis=-3)
    other_first = jnp.stack([other, x], axis=-3)
    return jnp.where((position & bit) == 0, mine_first, other_first)


def scatter_step(x, bit):
    position = lax.axis_index("dev")
    mine = ((position & bit) != 0).astype(jnp.int32)
    axis = x.ndim - 3
    kept = lax.dynamic_index_in_dim(x, mine, axis, keepdims=False)
    sent = lax.dynamic_index_in_dim(x, 1 - mine, axis, keepdims=False)
    other = exchange(sent.astype(bf16), bit)
    return kept.astype(f32) + other.astype(f32)


def all_bits():
    devices = lax.axis_size("dev")
    bits = []
    bit = devices // 2
    while bit:
        bits.append(bit)
        bit //= 2
    return bits


def gather_rows(x, early):
    bits = all_bits()
    width = x.shape[-1]
    mark = None
    for number, bit in enumerate(bits):
        x = gather_step(x, bit)
        if number + 1 == early:
            mark = x
    return x.reshape(-1, width), mark


def scatter_rows(x):
    bits = all_bits()
    devices = lax.axis_size("dev")
    width = x.shape[-1]
    x = x.reshape((2,) * len(bits) + (x.shape[0] // devices, width))
    for bit in reversed(bits):
        x = scatter_step(x, bit)
    return x


def body(
    peripheral, hubs, tiles, tile_rows, local_cols, tile_count, send_list, hub_place, w_in, w_out
):
    position = lax.axis_index("dev")
    block_size = tiles.shape[1]
    width = peripheral.shape[1]
    own_count = peripheral.shape[0] // block_size
    hub_rows = hub_place.shape[0]
    hub_count = hub_rows // block_size
    hub_local = hubs.shape[0]
    rows = jnp.where(tile_rows < hub_count, tile_rows, tile_rows - position * own_count)
    cols = jnp.where(local_cols < hub_count, local_cols, local_cols - position * own_count)
    remote_rows = rows[: send_list.shape[1]] - hub_count
    place_col = hub_place.reshape(hub_rows, 1)
    place_row = hub_place.reshape(1, hub_rows)
    mine_rows = (position * hub_local).astype(jnp.int32).reshape(1)
    own = peripheral.reshape(own_count, block_size, width)

    outgoing = pack(send_list, own)
    gathered, mark = gather_rows(hubs, 2)
    outgoing, mark = lax.optimization_barrier((outgoing, mark))
    incoming = lax.all_to_all(outgoing, "dev", split_axis=0, concat_axis=0, tiled=True)
    part, table = hub_first(rows, cols, tile_count, place_col, gathered, own, tiles)
    base = own_sums(rows, cols, tile_count, table, tiles, own_count)
    hub_sum = scatter_rows(part.reshape(hub_rows, width))
    hub_own = lax.dynamic_slice_in_dim(
        table[:hub_count].reshape(hub_rows, width), position * hub_local, hub_local, 0
    )
    hub_new = hub_network(hub_own, hub_sum, w_in[0], w_out[0])
    own, outgoing = peripheral_network(
        remote_rows, send_list, base, incoming, tiles, w_in[0], w_out[0], True
    )

    gathered, mark = gather_rows(hub_new, 2)
    outgoing, mark = lax.optimization_barrier((outgoing, mark))
    incoming = lax.all_to_all(outgoing, "dev", split_axis=0, concat_axis=0, tiled=True)
    part, hub_own, table = hub_second(
        rows,
        cols,
        tile_count,
        mine_rows,
        place_row,
        gathered.reshape(hub_count, block_size, width),
        own,
        tiles,
        hub_local,
    )
    base = own_sums(rows, cols, tile_count, table, tiles, own_count)
    hub_sum = scatter_rows(part)
    hub_out = hub_network(hub_own, hub_sum, w_in[1], w_out[1])
    (peri_out,) = peripheral_network(
        remote_rows, send_list, base, incoming, tiles, w_in[1], w_out[1], False
    )
    return (peri_out.reshape(peripheral.shape), hub_out)


def solution(mesh):
    in_specs = (
        P("dev", None),
        P("dev", None),
        P("dev", None, None),
        P("dev"),
        P("dev"),
        P("dev"),
        P("dev", None),
        P(),
        P(),
        P(),
    )
    out_specs = (P("dev", None), P("dev", None))
    return jax.shard_map(body, mesh=mesh, in_specs=in_specs, out_specs=out_specs, check_vma=False)
```

time: 680 us -> 286 us (0.42)
  waiting for transfers between devices: 353 us -> 88.2 us
  Pallas kernels: 0 us -> 137 us
  local copies, waits for them, and re-layouts: 126 us -> 7.5 us
  other arithmetic: 105 us -> 4.62 us
  matrix products: 67 us -> 0 us
  starting transfers between devices: 11.2 us -> 45.7 us
  between operations: 14.6 us -> 1.85 us
    psum x2 -> x0, waiting for transfers between devices: 256 us -> none  [body(): hub_sum = lax.psum(hub_part, 'dev')]
    pallas_call x0 -> x9, Pallas kernels: none -> 137 us  [the longest x1 65.6 us: pack(): pl.pallas_call(pack_kernel, out_shape=jax.ShapeDtypeStruct((devices,) + b...]
    gather x24 -> x0, local copies, waits for them, and re-layouts: 95.8 us -> none  [the longest x18 55.8 us: group_step(): column_table[col_group]]
    ppermute x0 -> x20, waiting for transfers between devices: none -> 88.2 us  [exchange(): return lax.ppermute(x, 'dev', [(i, i ^ bit) for i in range(devices)])]
    scatter-add x18 -> x0, other arithmetic: 81.4 us -> none  [group_step(): return carry.at[row_group].add(products * live_group[:, None, None])]
    dot_general x20 -> x0, matrix products: 67 us -> none  [the longest x2 40.7 us: feed_forward(): jnp.dot(hidden, second, preferred_element_type=jnp.float32)]
    all_gather x1 -> x0, waiting for transfers between devices: 58.5 us -> none  [body(): hub_full = lax.all_gather(hubs, 'dev', axis=0, tiled=True)]
    all_to_all x2, waiting for transfers between devices: 38.4 us -> 0.01 us  [body(): lax.all_to_all(outgoing, 'dev', split_axis=0, concat_axis=0, tiled=True)]
  transfers between devices with their start and end apart: 5 -> 22, of which waited for: 4 -> 16; matrix products, arithmetic and copies ran while one was open for 5% -> 4% of each run, Pallas kernels for 0% -> 38%
where the time goes in v1:
time: 286 us; the launch traced here: 285 us
  Pallas kernels  137 us (48%)
  waiting for transfers between devices  88.2 us (31%)
  starting transfers between devices  45.7 us (16%)
  local copies, waits for them, and re-layouts  7.5 us (3%)
  other arithmetic  4.62 us (2%)
    ppermute x20, waiting for transfers between devices, exchange(): return lax.ppermute(x, 'dev', [(i, i ^ bit) for i in range(devices)])  88.2 us
    pallas_call x1, Pallas kernels, pack(): pl.pallas_call(pack_kernel, out_shape=jax.ShapeDtypeStruct((devices,) + b...  65.6 us
    pallas_call x2, Pallas kernels, peripheral_network(): pl.pallas_call(functools.partial(network_kernel, 512, with_send), out_sha...  37.6 us
    ppermute x20, starting transfers between devices, exchange(): return lax.ppermute(x, 'dev', [(i, i ^ bit) for i in range(devices)])  33 us
    all_to_all x2, starting transfers between devices, body(): lax.all_to_all(outgoing, 'dev', split_axis=0, concat_axis=0, tiled=True)  12.7 us
    pallas_call x2, Pallas kernels, own_sums(): pl.pallas_call(own_kernel, out_shape=jax.ShapeDtypeStruct((own_count, blo...  12.6 us
    pallas_call x1, Pallas kernels, hub_first(): pl.pallas_call(hub_first_kernel, out_shape=(jax.ShapeDtypeStruct((hub_cou...  9.89 us
    pallas_call x1, Pallas kernels, hub_second(): pl.pallas_call(hub_second_kernel, out_shape=(jax.ShapeDtypeStruct((hub_co...  9.84 us
  transfers between devices with their start and end apart: 22, of which 16 were waited for; matrix products, arithmetic and copies ran while one was open for 4% of the time, Pallas kernels for 38%

profile of v1, /device:TPU:0, one launch (start us, length us, event | category | flops | bytes accessed | tf_op | source)
XLA Modules:
  0.0 285.3 jit_solution(653391090281451347)
XLA Ops:
  0.6 4.1 %collective-permute-start = (bf16[64,256]{1,0:T(8,128)(2,1)}, bf16[64,256]{1,0:T(8,128)(2,1)S(1)}, u32[]{:S(2)}, u32[]{:S(2)}) collective-permute-start(bf16[64,256]{1,0:T(8,128)(2,1)} %param.11), channel_id=1, source_target_pairs={{0,16},{1,17},{2,18},{3,19},{4,20},{5,21},{6,22},{7,23},{8,24},{9,... | collective-permute-start | bytes 98312 | tf_op jit(solution)/shard_map/ppermute | solution.py:311
  4.8 2.5 collective-permute-done
  19.3 4.6 %collective-permute-done.3 = bf16[2,2,2,64,256]{4,3,0,1,2:T(8,128)(2,1)S(1)} collective-permute-done((bf16[2,2,2,64,256]{4,3,0,1,2:T(8,128)(2,1)S(1)}, bf16[2,2,2,64,256]{4,3,0,1,2:T(8,128)(2,1)S(1)}, u32[]{:S(2)}, u32[]{:S(2)}) %collective-permute-start.3) | collective-permute-done | bytes 262176 | tf_op jit(solution)/shard_map/ppermute | solution.py:311
  26.2 9.9 %hub_first.1 = (bf16[16,128,256]{2,1,0:T(8,128)(2,1)S(1)}, bf16[48,128,256]{2,1,0:T(8,128)(2,1)}) custom-call(s32[144]{0:T(256)S(1)} %compare_select_fusion.rows, s32[112]{0:T(128)S(1)} %compare_select_fusion.1.cols, s32[1]{0:T(128)S(6)} %copy.36.count, s32[2048,1]{1,0:T(8,128)S(1)} %copy.18.place_col, bf16[2048,256]{1,0:T(8,128)(2,1)S(1)} %bitcast.112, ...), custom_call_target="tpu_custom_call" | custom-call | tf_op jit(solution)/shard_map/hub_first/pallas_call | solution.py:120
  36.3 65.6 %pack.1 = bf16[32,128,256]{2,1,0:T(8,128)(2,1)} custom-call(s32[1,32]{1,0:T(1,128)} %chosen.5, bf16[32,128,256]{2,1,0:T(8,128)(2,1)} %bitcast.122), custom_call_target="tpu_custom_call" | custom-call | tf_op jit(solution)/shard_map/pack/pallas_call | solution.py:94
  101.9 8.2 %all-to-all-start = ((bf16[32,128,256]{2,1,0:T(8,128)(2,1)}), bf16[32,128,256]{2,1,0:T(8,128)(2,1)}, u32[]{:S(2)}, u32[]{:S(2)}) async-start(bf16[32,128,256]{2,1,0:T(8,128)(2,1)} %pack.1), calls=%async_computation | async-start | bytes 4194304 | tf_op jit(solution)/shard_map/all_to_all | solution.py:384
  112.1 19.9 %collective-permute-done.6 = bf16[2,2,2,64,256]{4,3,0,1,2:T(8,128)(2,1)S(1)} collective-permute-done((bf16[2,2,2,64,256]{4,3,0,1,2:T(8,128)(2,1)S(1)}, bf16[2,2,2,64,256]{4,3,0,1,2:T(8,128)(2,1)S(1)}, u32[]{:S(2)}, u32[]{:S(2)}) %collective-permute-start.6) | collective-permute-done | bytes 262176 | tf_op jit(solution)/shard_map/ppermute | solution.py:311
  132.1 6.2 %collective-permute-start.7 = (bf16[2,2,64,256]{3,2,0,1:T(8,128)(2,1)S(1)}, bf16[2,2,64,256]{3,2,0,1:T(8,128)(2,1)S(1)}, u32[]{:S(2)}, u32[]{:S(2)}) collective-permute-start(bf16[2,2,64,256]{3,2,0,1:T(8,128)(2,1)S(1)} %fusion.2), channel_id=1, source_target_pairs={{0,4},{1,5},{2,6},{3,7},{4,0},{5,1},{6,2},{7,3},{8,12},{9,13},{10,... | collective-permute-start | bytes 393224 | tf_op jit(solution)/shard_map/ppermute | solution.py:311
  140.1 3.1 %collective-permute-done.7 = bf16[2,2,64,256]{3,2,0,1:T(8,128)(2,1)S(1)} collective-permute-done((bf16[2,2,64,256]{3,2,0,1:T(8,128)(2,1)S(1)}, bf16[2,2,64,256]{3,2,0,1:T(8,128)(2,1)S(1)}, u32[]{:S(2)}, u32[]{:S(2)}) %collective-permute-start.7) | collective-permute-done | bytes 131104 | tf_op jit(solution)/shard_map/ppermute | solution.py:311
  143.9 2.7 slice_bitcast_fusion
  148.5 2.9 %collective-permute-start.9 = (bf16[64,256]{1,0:T(8,128)(2,1)S(1)}, bf16[64,256]{1,0:T(8,128)(2,1)S(1)}, u32[]{:S(2)}, u32[]{:S(2)}) collective-permute-start(bf16[64,256]{1,0:T(8,128)(2,1)S(1)} %fusion.7), channel_id=1, source_target_pairs={{0,16},{1,17},{2,18},{3,19},{4,20},{5,21},{6,22},{7,23},{8,24},{9,... | collective-permute-start | bytes 98312 | tf_op jit(solution)/shard_map/ppermute | solution.py:311
  151.4 8.9 %collective-permute-done.9 = bf16[64,256]{1,0:T(8,128)(2,1)S(1)} collective-permute-done((bf16[64,256]{1,0:T(8,128)(2,1)S(1)}, bf16[64,256]{1,0:T(8,128)(2,1)S(1)}, u32[]{:S(2)}, u32[]{:S(2)}) %collective-permute-start.9) | collective-permute-done | bytes 32800 | tf_op jit(solution)/shard_map/ppermute | solution.py:311
  161.1 6.3 %own_sums.2.base = f32[32,128,256]{2,1,0:T(8,128)} custom-call(s32[144]{0:T(256)S(1)} %compare_select_fusion.rows, s32[112]{0:T(128)S(1)} %compare_select_fusion.1.cols, s32[1]{0:T(128)S(6)} %copy.36.count, bf16[48,128,256]{2,1,0:T(8,128)(2,1)S(1)} %copy-done.1, bf16[144,128,128]{2,1,0:T(8,128)(2,1)} %tiles.11), custom_call_target="tpu_custom_call" | custom-call | tf_op jit(solution)/shard_map/own_sums/pallas_call | solution.py:198
  168.7 3.0 %collective-permute-done.11 = bf16[2,64,256]{2,1,0:T(8,128)(2,1)S(1)} collective-permute-done((bf16[2,64,256]{2,1,0:T(8,128)(2,1)S(1)}, bf16[2,64,256]{2,1,0:T(8,128)(2,1)S(1)}, u32[]{:S(2)}, u32[]{:S(2)}) %collective-permute-start.11) | collective-permute-done | bytes 65568 | tf_op jit(solution)/shard_map/ppermute | solution.py:311
  173.4 19.1 %peripheral_network.2 = (bf16[32,128,256]{2,1,0:T(8,128)(2,1)}, bf16[32,128,256]{2,1,0:T(8,128)(2,1)}) custom-call(s32[32]{0:T(128)S(1)} %slice_add_fusion.rows, s32[1,32]{1,0:T(1,128)S(1)} %copy-done.4, f32[32,128,256]{2,1,0:T(8,128)} %own_sums.2.base, bf16[32,128,256]{2,1,0:T(8,128)(2,1)} %all-to-all-done.incoming, bf16[144,128,128]{2,1,0:T(8,128)(2,1)} %tiles.11, ...), custom_call_target="tpu_custom_call" | custom-call | tf_op jit(solution)/shard_map/peripheral_network/pallas_call | solution.py:290
  192.5 4.5 %all-to-all-start.1 = ((bf16[32,128,256]{2,1,0:T(8,128)(2,1)}), bf16[32,128,256]{2,1,0:T(8,128)(2,1)}, u32[]{:S(2)}, u32[]{:S(2)}) async-start(bf16[32,128,256]{2,1,0:T(8,128)(2,1)} %get-tuple-element.17), calls=%async_computation.1 | async-start | bytes 4194304 | tf_op jit(solution)/shard_map/all_to_all | solution.py:398
  198.9 20.0 %collective-permute-done.13 = bf16[2,2,2,64,256]{4,3,0,1,2:T(8,128)(2,1)S(1)} collective-permute-done((bf16[2,2,2,64,256]{4,3,0,1,2:T(8,128)(2,1)S(1)}, bf16[2,2,2,64,256]{4,3,0,1,2:T(8,128)(2,1)S(1)}, u32[]{:S(2)}, u32[]{:S(2)}) %collective-permute-start.13) | collective-permute-done | bytes 262176 | tf_op jit(solution)/shard_map/ppermute | solution.py:311
  221.2 9.8 %hub_second.1 = (bf16[2048,256]{1,0:T(8,128)(2,1)S(1)}, bf16[64,256]{1,0:T(8,128)(2,1)S(1)}, bf16[48,128,256]{2,1,0:T(8,128)(2,1)}) custom-call(s32[144]{0:T(256)S(1)} %compare_select_fusion.rows, s32[112]{0:T(128)S(1)} %compare_select_fusion.1.cols, s32[1]{0:T(128)S(6)} %copy.36.count, s32[1]{0:T(128)} %bitcast.mine_rows, s32[1,2048]{1,0:T(1,128)S(1)} %bitcast.120, ...), custom_call_target="tpu_custom_call" | custom-call | tf_op jit(solution)/shard_map/hub_second/pallas_call | solution.py:166
  235.7 9.6 %collective-permute-done.16 = bf16[2,2,2,64,256]{4,3,0,1,2:T(8,128)(2,1)S(1)} collective-permute-done((bf16[2,2,2,64,256]{4,3,0,1,2:T(8,128)(2,1)S(1)}, bf16[2,2,2,64,256]{4,3,0,1,2:T(8,128)(2,1)S(1)}, u32[]{:S(2)}, u32[]{:S(2)}) %collective-permute-start.16) | collective-permute-done | bytes 262176 | tf_op jit(solution)/shard_map/ppermute | solution.py:311
  245.5 6.0 %collective-permute-start.17 = (bf16[2,2,64,256]{3,2,0,1:T(8,128)(2,1)S(1)}, bf16[2,2,64,256]{3,2,0,1:T(8,128)(2,1)S(1)}, u32[]{:S(2)}, u32[]{:S(2)}) collective-permute-start(bf16[2,2,64,256]{3,2,0,1:T(8,128)(2,1)S(1)} %fusion.3), channel_id=1, source_target_pairs={{0,4},{1,5},{2,6},{3,7},{4,0},{5,1},{6,2},{7,3},{8,12},{9,13},{10,... | collective-permute-start | bytes 393224 | tf_op jit(solution)/shard_map/ppermute | solution.py:311
  251.5 3.2 %collective-permute-done.17 = bf16[2,2,64,256]{3,2,0,1:T(8,128)(2,1)S(1)} collective-permute-done((bf16[2,2,64,256]{3,2,0,1:T(8,128)(2,1)S(1)}, bf16[2,2,64,256]{3,2,0,1:T(8,128)(2,1)S(1)}, u32[]{:S(2)}, u32[]{:S(2)}) %collective-permute-start.17) | collective-permute-done | bytes 131104 | tf_op jit(solution)/shard_map/ppermute | solution.py:311
  254.8 4.3 %collective-permute-done.18 = bf16[2,64,256]{2,1,0:T(8,128)(2,1)S(1)} collective-permute-done((bf16[2,64,256]{2,1,0:T(8,128)(2,1)S(1)}, bf16[2,64,256]{2,1,0:T(8,128)(2,1)S(1)}, u32[]{:S(2)}, u32[]{:S(2)}) %collective-permute-start.18) | collective-permute-done | bytes 65568 | tf_op jit(solution)/shard_map/ppermute | solution.py:311
  259.2 6.3 %own_sums.3.base = f32[32,128,256]{2,1,0:T(8,128)} custom-call(s32[144]{0:T(256)S(1)} %compare_select_fusion.rows, s32[112]{0:T(128)S(1)} %compare_select_fusion.1.cols, s32[1]{0:T(128)S(6)} %copy.36.count, bf16[48,128,256]{2,1,0:T(8,128)(2,1)S(1)} %copy-done.2, bf16[144,128,128]{2,1,0:T(8,128)(2,1)} %tiles.11), custom_call_target="tpu_custom_call" | custom-call | tf_op jit(solution)/shard_map/own_sums/pallas_call | solution.py:198
  266.8 18.5 %peripheral_network.3 = bf16[32,128,256]{2,1,0:T(8,128)(2,1)} custom-call(s32[32]{0:T(128)S(1)} %slice_add_fusion.rows, s32[1,32]{1,0:T(1,128)S(1)} %copy-done.4, f32[32,128,256]{2,1,0:T(8,128)} %own_sums.3.base, bf16[32,128,256]{2,1,0:T(8,128)(2,1)} %all-to-all-done.1.incoming, bf16[144,128,128]{2,1,0:T(8,128)(2,1)} %tiles.11, ...), custom_call_target="tpu_custom_call" | custom-call | tf_op jit(solution)/shard_map/peripheral_network/pallas_call | solution.py:290
  (99 shorter events, 34.1 us)
Async XLA Ops:
  0.6 24.1 %copy-start.3 = (s32[2048]{0:T(1024)S(1)}, s32[2048]{0:T(1024)}, u32[]{:S(2)}) copy-start(s32[2048]{0:T(1024)} %param.17) | copy-start | bytes 24580
  0.6 6.6 %collective-permute-start = (bf16[64,256]{1,0:T(8,128)(2,1)}, bf16[64,256]{1,0:T(8,128)(2,1)S(1)}, u32[]{:S(2)}, u32[]{:S(2)}) collective-permute-start(bf16[64,256]{1,0:T(8,128)(2,1)} %param.11), channel_id=1, source_target_pairs={{0,16},{1,17},{2,18},{3,19},{4,20},{5,21},{6,22},{7,23},{8,24},{9,... | collective-permute-start | bytes 98312 | tf_op jit(solution)/shard_map/ppermute | solution.py:311
  8.1 4.3 %collective-permute-start.1 = (bf16[2,64,256]{2,1,0:T(8,128)(2,1)S(1)}, bf16[2,64,256]{2,1,0:T(8,128)(2,1)S(1)}, u32[]{:S(2)}, u32[]{:S(2)}) collective-permute-start(bf16[2,64,256]{2,1,0:T(8,128)(2,1)S(1)} %maximum_select_fusion.14), channel_id=1, source_target_pairs={{0,8},{1,9},{2,10},{3,11},{4,12},{5,13},{6,14},{7,15},{8,0},{9,1},... | collective-permute-start | bytes 196616 | tf_op jit(solution)/shard_map/ppermute | solution.py:311
  12.4 5.0 %collective-permute-start.2 = (bf16[2,2,64,256]{3,2,0,1:T(8,128)(2,1)S(1)}, bf16[2,2,64,256]{3,2,0,1:T(8,128)(2,1)S(1)}, u32[]{:S(2)}, u32[]{:S(2)}) collective-permute-start(bf16[2,2,64,256]{3,2,0,1:T(8,128)(2,1)S(1)} %maximum_select_fusion.11), channel_id=1, source_target_pairs={{0,4},{1,5},{2,6},{3,7},{4,0},{5,1},{6,2},{7,3},{8,12},{9,13},{10,... | collective-permute-start | bytes 393224 | tf_op jit(solution)/shard_map/ppermute | solution.py:311
  17.5 6.4 %collective-permute-start.3 = (bf16[2,2,2,64,256]{4,3,0,1,2:T(8,128)(2,1)S(1)}, bf16[2,2,2,64,256]{4,3,0,1,2:T(8,128)(2,1)S(1)}, u32[]{:S(2)}, u32[]{:S(2)}) collective-permute-start(bf16[2,2,2,64,256]{4,3,0,1,2:T(8,128)(2,1)S(1)} %maximum_select_fusion.7), channel_id=1, source_target_pairs={{0,2},{1,3},{2,0},{3,1},{4,6},{5,7},{6,4},{7,5},{8,10},{9,11},{10,... | collective-permute-start | bytes 786440 | tf_op jit(solution)/shard_map/ppermute | solution.py:311
  24.0 2.0 collective-permute-start.4
  36.2 73.9 %collective-permute-start.5 = (bf16[2,2,2,2,64,256]{5,4,0,1,2,3:T(8,128)(2,1)S(1)}, bf16[2,2,2,2,64,256]{5,4,0,1,2,3:T(8,128)(2,1)S(1)}, u32[]{:S(2)}, u32[]{:S(2)}) collective-permute-start(bf16[2,2,2,2,64,256]{5,4,0,1,2,3:T(8,128)(2,1)S(1)} %bitcast.143), channel_id=1, source_target_pairs={{0,1},{1,0},{2,3},{3,2},{4,5},{5,4},{6,7},{7,6},{8,9},{9,8},{10,11... | collective-permute-start | bytes 1572872 | tf_op jit(solution)/shard_map/ppermute | solution.py:311
  101.9 71.5 %all-to-all-start = ((bf16[32,128,256]{2,1,0:T(8,128)(2,1)}), bf16[32,128,256]{2,1,0:T(8,128)(2,1)}, u32[]{:S(2)}, u32[]{:S(2)}) async-start(bf16[32,128,256]{2,1,0:T(8,128)(2,1)} %pack.1), calls=%async_computation | async-start | bytes 4194304 | tf_op jit(solution)/shard_map/all_to_all | solution.py:384
  110.4 21.7 %collective-permute-start.6 = (bf16[2,2,2,64,256]{4,3,0,1,2:T(8,128)(2,1)S(1)}, bf16[2,2,2,64,256]{4,3,0,1,2:T(8,128)(2,1)S(1)}, u32[]{:S(2)}, u32[]{:S(2)}) collective-permute-start(bf16[2,2,2,64,256]{4,3,0,1,2:T(8,128)(2,1)S(1)} %fusion), channel_id=1, source_target_pairs={{0,2},{1,3},{2,0},{3,1},{4,6},{5,7},{6,4},{7,5},{8,10},{9,11},{10,... | collective-permute-start | bytes 786440 | tf_op jit(solution)/shard_map/ppermute | solution.py:311
  132.1 11.1 %collective-permute-start.7 = (bf16[2,2,64,256]{3,2,0,1:T(8,128)(2,1)S(1)}, bf16[2,2,64,256]{3,2,0,1:T(8,128)(2,1)S(1)}, u32[]{:S(2)}, u32[]{:S(2)}) collective-permute-start(bf16[2,2,64,256]{3,2,0,1:T(8,128)(2,1)S(1)} %fusion.2), channel_id=1, source_target_pairs={{0,4},{1,5},{2,6},{3,7},{4,0},{5,1},{6,2},{7,3},{8,12},{9,13},{10,... | collective-permute-start | bytes 393224 | tf_op jit(solution)/shard_map/ppermute | solution.py:311
  143.9 4.6 %collective-permute-start.8 = (bf16[2,64,256]{2,1,0:T(8,128)(2,1)}, bf16[2,64,256]{2,1,0:T(8,128)(2,1)S(1)}, u32[]{:S(2)}, u32[]{:S(2)}) collective-permute-start(bf16[2,64,256]{2,1,0:T(8,128)(2,1)} %fusion.4), channel_id=1, source_target_pairs={{0,8},{1,9},{2,10},{3,11},{4,12},{5,13},{6,14},{7,15},{8,0},{9,1},... | collective-permute-start | bytes 196616 | tf_op jit(solution)/shard_map/ppermute | solution.py:311
  148.5 11.8 %collective-permute-start.9 = (bf16[64,256]{1,0:T(8,128)(2,1)S(1)}, bf16[64,256]{1,0:T(8,128)(2,1)S(1)}, u32[]{:S(2)}, u32[]{:S(2)}) collective-permute-start(bf16[64,256]{1,0:T(8,128)(2,1)S(1)} %fusion.7), channel_id=1, source_target_pairs={{0,16},{1,17},{2,18},{3,19},{4,20},{5,21},{6,22},{7,23},{8,24},{9,... | collective-permute-start | bytes 98312 | tf_op jit(solution)/shard_map/ppermute | solution.py:311
  161.0 6.4 %collective-permute-start.10 = (bf16[64,256]{1,0:T(8,128)(2,1)S(1)}, bf16[64,256]{1,0:T(8,128)(2,1)S(1)}, u32[]{:S(2)}, u32[]{:S(2)}) collective-permute-start(bf16[64,256]{1,0:T(8,128)(2,1)S(1)} %hub_network.2), channel_id=1, source_target_pairs={{0,16},{1,17},{2,18},{3,19},{4,20},{5,21},{6,22},{7,23},{8,24},{9,... | collective-permute-start | bytes 98312 | tf_op jit(solution)/shard_map/ppermute | solution.py:311
  167.4 4.3 %collective-permute-start.11 = (bf16[2,64,256]{2,1,0:T(8,128)(2,1)S(1)}, bf16[2,64,256]{2,1,0:T(8,128)(2,1)S(1)}, u32[]{:S(2)}, u32[]{:S(2)}) collective-permute-start(bf16[2,64,256]{2,1,0:T(8,128)(2,1)S(1)} %maximum_select_fusion.16), channel_id=1, source_target_pairs={{0,8},{1,9},{2,10},{3,11},{4,12},{5,13},{6,14},{7,15},{8,0},{9,1},... | collective-permute-start | bytes 196616 | tf_op jit(solution)/shard_map/ppermute | solution.py:311
  172.4 24.7 %collective-permute-start.12 = (bf16[2,2,64,256]{3,2,0,1:T(8,128)(2,1)}, bf16[2,2,64,256]{3,2,0,1:T(8,128)(2,1)S(1)}, u32[]{:S(2)}, u32[]{:S(2)}) collective-permute-start(bf16[2,2,64,256]{3,2,0,1:T(8,128)(2,1)} %maximum_select_fusion.13), channel_id=1, source_target_pairs={{0,4},{1,5},{2,6},{3,7},{4,0},{5,1},{6,2},{7,3},{8,12},{9,13},{10,... | collective-permute-start | bytes 393224 | tf_op jit(solution)/shard_map/ppermute | solution.py:311
  192.5 74.3 %all-to-all-start.1 = ((bf16[32,128,256]{2,1,0:T(8,128)(2,1)}), bf16[32,128,256]{2,1,0:T(8,128)(2,1)}, u32[]{:S(2)}, u32[]{:S(2)}) async-start(bf16[32,128,256]{2,1,0:T(8,128)(2,1)} %get-tuple-element.17), calls=%async_computation.1 | async-start | bytes 4194304 | tf_op jit(solution)/shard_map/all_to_all | solution.py:398
  197.1 21.8 %collective-permute-start.13 = (bf16[2,2,2,64,256]{4,3,0,1,2:T(8,128)(2,1)S(1)}, bf16[2,2,2,64,256]{4,3,0,1,2:T(8,128)(2,1)S(1)}, u32[]{:S(2)}, u32[]{:S(2)}) collective-permute-start(bf16[2,2,2,64,256]{4,3,0,1,2:T(8,128)(2,1)S(1)} %maximum_select_fusion.9), channel_id=1, source_target_pairs={{0,2},{1,3},{2,0},{3,1},{4,6},{5,7},{6,4},{7,5},{8,10},{9,11},{10,... | collective-permute-start | bytes 786440 | tf_op jit(solution)/shard_map/ppermute | solution.py:311
  219.0 2.0 collective-permute-start.14
  231.2 2.0 collective-permute-start.15
  233.4 25.8 %copy-start.2 = (bf16[48,128,256]{2,1,0:T(8,128)(2,1)S(1)}, bf16[48,128,256]{2,1,0:T(8,128)(2,1)}, u32[]{:S(2)}) copy-start(bf16[48,128,256]{2,1,0:T(8,128)(2,1)} %get-tuple-element.15.table) | copy-start | bytes 9437188
  233.4 12.0 %collective-permute-start.16 = (bf16[2,2,2,64,256]{4,3,0,1,2:T(8,128)(2,1)S(1)}, bf16[2,2,2,64,256]{4,3,0,1,2:T(8,128)(2,1)S(1)}, u32[]{:S(2)}, u32[]{:S(2)}) collective-permute-start(bf16[2,2,2,64,256]{4,3,0,1,2:T(8,128)(2,1)S(1)} %fusion.1), channel_id=1, source_target_pairs={{0,2},{1,3},{2,0},{3,1},{4,6},{5,7},{6,4},{7,5},{8,10},{9,11},{10,... | collective-permute-start | bytes 786440 | tf_op jit(solution)/shard_map/ppermute | solution.py:311
  245.5 9.2 %collective-permute-start.17 = (bf16[2,2,64,256]{3,2,0,1:T(8,128)(2,1)S(1)}, bf16[2,2,64,256]{3,2,0,1:T(8,128)(2,1)S(1)}, u32[]{:S(2)}, u32[]{:S(2)}) collective-permute-start(bf16[2,2,64,256]{3,2,0,1:T(8,128)(2,1)S(1)} %fusion.3), channel_id=1, source_target_pairs={{0,4},{1,5},{2,6},{3,7},{4,0},{5,1},{6,2},{7,3},{8,12},{9,13},{10,... | collective-permute-start | bytes 393224 | tf_op jit(solution)/shard_map/ppermute | solution.py:311
  254.7 4.3 %collective-permute-start.18 = (bf16[2,64,256]{2,1,0:T(8,128)(2,1)S(1)}, bf16[2,64,256]{2,1,0:T(8,128)(2,1)S(1)}, u32[]{:S(2)}, u32[]{:S(2)}) collective-permute-start(bf16[2,64,256]{2,1,0:T(8,128)(2,1)S(1)} %fusion.5), channel_id=1, source_target_pairs={{0,8},{1,9},{2,10},{3,11},{4,12},{5,13},{6,14},{7,15},{8,0},{9,1},... | collective-permute-start | bytes 196616 | tf_op jit(solution)/shard_map/ppermute | solution.py:311
  259.1 6.4 %collective-permute-start.19 = (bf16[64,256]{1,0:T(8,128)(2,1)S(1)}, bf16[64,256]{1,0:T(8,128)(2,1)S(1)}, u32[]{:S(2)}, u32[]{:S(2)}) collective-permute-start(bf16[64,256]{1,0:T(8,128)(2,1)S(1)} %fusion.8), channel_id=1, source_target_pairs={{0,16},{1,17},{2,18},{3,19},{4,20},{5,21},{6,22},{7,23},{8,24},{9,... | collective-permute-start | bytes 98312 | tf_op jit(solution)/shard_map/ppermute | solution.py:311
  (5 other events, 72.0 us)
